TPU v7x, 512 devices: a whole 4x4x16 slice. The times are simulated.
512 devices in a mesh: segment: 4 (over y_lo, core), ctx: 32 (over z, y_hi), head: 4 (over x).
Axes of the slice: x: 4, y: 4 (y_hi: 2, y_lo: 2; y = y_hi * 2 + y_lo), z: 16, core: 2. Of those that a mesh axis runs over, the one named last changes fastest.
Arguments:
- hidden: bfloat16 [4, 8192, 2880], P('segment', 'ctx', 'head'), may hold values from -450 to 450
- merge_weight: bfloat16 [3, 2880, 2880], P(None, 'head', 'segment'), may hold values from -0.0625 to 0.0625
- query_weight: bfloat16 [5760, 2048], P('ctx', ('segment', 'head')), may hold values from -1 to 1
- key_weight: bfloat16 [5760, 256], P('ctx', 'segment'), may hold values from -8 to 8
- value_weight: bfloat16 [5760, 256], P('ctx', 'segment'), may hold values from -0.078125 to 0.078125
- block_order: int32 [64], replicated, may hold values from 0 to 63, each once
Outputs:
- attended: bfloat16 [8192, 2048], P('ctx', ('segment', 'head'))
Inputs may be any that keep to these rules, and one draw needn't show every extreme that they name: `block_order`: a permutation of the sequence blocks.
All inputs are finite; a program needn't handle non-finite values.
Results may differ from a plain program's by a relative error of at most 0.023.
The roundings to bfloat16 on the way count: a program that leaves them out, or rounds other values in their place, can miss the bound.
Values may be sent and summed in bfloat16 or wider, within the bound.
No kernel may reach another device: no remote copies, remote signals or barrier semaphores. Data moves between devices by JAX's collectives and lax.ppermute only.
A program may use at most 64 MiB of HBM per device.

v0:
```python
import math
import jax
import jax.numpy as jnp
from jax import lax
from jax.sharding import PartitionSpec as P

HD = 64


def normalize(matrix):
    widened = matrix.astype(jnp.float32)
    return widened * lax.rsqrt(jnp.mean(widened * widened, axis=-1, keepdims=True) + 1e-06)


def seq_positions(row_ids, order, block_len):
    block_ids = jnp.arange(order.shape[0], dtype=jnp.int32)
    matches = (row_ids // block_len)[:, None] == block_ids[None, :]
    block_first = jnp.sum(jnp.where(matches, order[None, :], 0), axis=1)
    return block_first * block_len + row_ids % block_len


def attend_block(carry, query_heads, query_pos, key_blk, value_blk, key_pos):
    run_max, run_total, accum = carry
    tok_rows, heads_count, head_size = query_heads.shape
    scores = (
        jnp.einsum("tgd,nd->tgn", query_heads, key_blk, preferred_element_type=jnp.float32) * 0.125
    )
    allowed = key_pos[None, None, :] <= query_pos[:, None, None]
    scores = jnp.where(allowed, scores, -1e30)
    new_max = jnp.maximum(run_max, jnp.max(scores, axis=2))
    rescale = jnp.exp(run_max - new_max)
    unscaled = jnp.where(allowed, jnp.exp(scores - new_max[:, :, None]), 0.0)
    run_total = run_total * rescale + jnp.sum(unscaled, axis=2)
    mixed_rows = jnp.einsum(
        "tgn,nd->tgd", unscaled.astype(jnp.bfloat16), value_blk, preferred_element_type=jnp.float32
    )
    grown = accum.reshape(tok_rows, heads_count, head_size) * rescale[:, :, None] + mixed_rows
    return (new_max, run_total, grown.reshape(tok_rows, heads_count * head_size))


def body(hidden, merge_weight, query_weight, key_weight, value_weight, block_order):
    tok_rows = hidden.shape[1]
    block_len = tok_rows // 2
    segments = lax.axis_size("segment")
    heads_here = lax.axis_size("head")
    segment_id = lax.axis_index("segment")
    head_id = lax.axis_index("head")
    ctx_id = lax.axis_index("ctx")
    sections = lax.all_gather(hidden, "segment", axis=0, tiled=True)
    partial_value = jnp.einsum(
        "ktf,kfc->tc", sections[:3], merge_weight, preferred_element_type=jnp.float32
    )
    col_piece = partial_value.shape[1] // heads_here
    summed = lax.psum(partial_value, "head")
    merged_part = lax.dynamic_slice_in_dim(summed, head_id * col_piece, col_piece, 1)
    merged_part = merged_part.astype(jnp.bfloat16)
    embed_part = lax.dynamic_slice_in_dim(sections[3], segment_id * col_piece, col_piece, 1)
    merged_all, embed_mixed = (
        lax.all_gather(merged_part, ("segment", "head"), axis=1, tiled=True),
        lax.all_gather(embed_part, ("segment", "head"), axis=1, tiled=True),
    )
    embed_all = embed_mixed.reshape(tok_rows, segments, heads_here, col_piece).transpose(0, 2, 1, 3)
    embed_all = embed_all.reshape(tok_rows, segments * heads_here * col_piece)
    draft_input = jnp.concatenate([normalize(embed_all), normalize(merged_all)], axis=1).astype(
        jnp.bfloat16
    )
    query_piece = lax.all_gather(query_weight, "ctx", axis=0, tiled=True)
    key_piece = lax.all_gather(key_weight, "ctx", axis=0, tiled=True)
    value_piece = lax.all_gather(value_weight, "ctx", axis=0, tiled=True)
    query_acc = jnp.dot(draft_input, query_piece, preferred_element_type=jnp.float32)
    key_acc = jnp.dot(draft_input, key_piece, preferred_element_type=jnp.float32)
    value_acc = jnp.dot(draft_input, value_piece, preferred_element_type=jnp.float32)
    query_acc, key_acc, value_acc = (query_acc, key_acc, value_acc)
    query_heads = query_acc.astype(jnp.bfloat16).reshape(tok_rows, -1, HD)
    key_vectors = key_acc.astype(jnp.bfloat16)
    value_vectors = value_acc.astype(jnp.bfloat16)
    heads_count = query_heads.shape[1]
    query_pos = seq_positions(
        ctx_id * tok_rows + jnp.arange(tok_rows, dtype=jnp.int32), block_order, block_len
    )
    initial_attn = (
        jnp.full((tok_rows, heads_count), -1e30, jnp.float32),
        jnp.zeros((tok_rows, heads_count), jnp.float32),
        jnp.zeros((tok_rows, heads_count * HD), jnp.float32),
    )
    key_piece = lax.all_gather(key_vectors, "ctx", axis=0, tiled=True)
    value_piece = lax.all_gather(value_vectors, "ctx", axis=0, tiled=True)
    row_count = key_piece.shape[0]
    key_step = math.gcd(row_count, 512)

    def one_block(turn_index, carried):
        offset = turn_index * key_step
        key_blk = lax.dynamic_slice_in_dim(key_piece, offset, key_step, 0)
        value_blk = lax.dynamic_slice_in_dim(value_piece, offset, key_step, 0)
        key_pos = seq_positions(
            offset + jnp.arange(key_step, dtype=jnp.int32), block_order, block_len
        )
        return attend_block(carried, query_heads, query_pos, key_blk, value_blk, key_pos)

    run_max, run_total, accum = lax.fori_loop(0, row_count // key_step, one_block, initial_attn)
    output = accum.reshape(tok_rows, heads_count, HD) / run_total[:, :, None]
    return output.reshape(tok_rows, heads_count * HD).astype(jnp.bfloat16)


def solution(mesh):
    return jax.shard_map(
        body,
        mesh=mesh,
        in_specs=(
            P("segment", "ctx", "head"),
            P(None, "head", "segment"),
            P("ctx", ("segment", "head")),
            P("ctx", "segment"),
            P("ctx", "segment"),
            P(),
        ),
        out_specs=P("ctx", ("segment", "head")),
        check_vma=False,
    )
```

profile of v0, /device:TPU:4, one launch (start us, length us, event | category | flops | bytes accessed | tf_op | source)
XLA Modules:
  0.0 691.7 jit_solution(7909298819602587909)
XLA Ops:
  7.3 38.2 %all-gather.12.cloned.1.call-done = bf16[4,256,720]{1,2,0:T(8,128)(2,1)} async-done(((bf16[1,256,720]{1,2,0:T(8,128)(2,1)}), bf16[4,256,720]{1,2,0:T(8,128)(2,1)}) %all-gather.12.cloned.1.call-update) | async-done | bytes 1474576 | tf_op jit(solution)/shard_map/all_gather | solution.py:49
  47.5 3.6 convolution_bitcast_fusion
  51.1 25.7 %all-reduce.1 = bf16[256,720]{0,1:T(8,128)(2,1)} all-reduce(f32[256,720]{0,1:T(8,128)} %convolution_bitcast_fusion), channel_id=1, replica_groups=mesh['segment'=4,'ctx'=32,'head'=4] {'head'}, use_global_device_ids=true, to_apply=%region_1.0 | all-reduce | flops 184320 | bytes 1105920 | tf_op jit(solution)/shard_map/psum | solution.py:54
  79.0 83.5 %all-gather.4 = bf16[32,180,64]{1,2,0:T(8,128)(2,1)S(1)} all-gather(bf16[1,180,64]{1,2,0:T(8,128)(2,1)S(1)} %bitcast.59), channel_id=1, replica_groups=mesh['segment'=4,'ctx'=32,'head'=4] {'ctx'}, dimensions={0}, use_global_device_ids=true | all-gather | bytes 760320 | tf_op jit(solution)/shard_map/all_gather | solution.py:69
  164.1 3.1 reshape.158
  167.2 31.9 %multiply_reduce_fusion.1 = (f32[256]{0:T(256)S(1)}, f32[256,2880]{0,1:T(8,128)}) fusion(bf16[1,256,2880]{1,0,2:T(2,128)(2,1)} %all-gather.18.cloned.1.call-done), kind=kLoop, calls=%fused_computation.39 | loop fusion | flops 2211584 | bytes 4424704 | tf_op jit(solution)/shard_map/reduce_sum | solution.py:12
  199.1 4.0 reshape.145
  203.2 3.8 copy.26
  207.0 4.1 reshape.144
  211.1 3.4 reshape.159
  214.5 2.4 multiply_reduce_fusion
  222.4 78.1 %all-gather.2 = bf16[32,180,64]{1,2,0:T(8,128)(2,1)S(1)} all-gather(bf16[1,180,64]{1,2,0:T(8,128)(2,1)S(1)} %bitcast.60), channel_id=1, replica_groups=mesh['segment'=4,'ctx'=32,'head'=4] {'ctx'}, dimensions={0}, use_global_device_ids=true | all-gather | bytes 760320 | tf_op jit(solution)/shard_map/all_gather | solution.py:68
  302.0 3.2 reshape.154
  305.2 3.3 convolution_convert_fusion.2
  308.7 9.7 %all-gather.22.cloned.1.call-done = bf16[32,180,128]{2,1,0:T(8,128)(2,1)} async-done(((bf16[1,180,128]{2,1,0:T(8,128)(2,1)}), bf16[32,180,128]{2,1,0:T(8,128)(2,1)}) %all-gather.22.cloned.1.call-update) | async-done | bytes 1474576 | tf_op jit(solution)/shard_map/all_gather | solution.py:67
  318.4 3.3 reshape.156
  321.7 3.0 convolution_convert_fusion
  324.7 127.4 %all-gather.16.cloned.1.call-done = bf16[8192,64]{0,1:T(8,128)(2,1)} async-done(((bf16[256,64]{0,1:T(8,128)(2,1)}), bf16[8192,64]{0,1:T(8,128)(2,1)}) %all-gather.16.cloned.1.call-update) | async-done | bytes 1048592 | tf_op jit(solution)/shard_map/all_gather | solution.py:87
  452.1 132.5 %all-gather.14.cloned.1.call-done = bf16[8192,64]{0,1:T(8,128)(2,1)} async-done(((bf16[256,64]{0,1:T(8,128)(2,1)}), bf16[8192,64]{0,1:T(8,128)(2,1)}) %all-gather.14.cloned.1.call-update) | async-done | bytes 1048592 | tf_op jit(solution)/shard_map/all_gather | solution.py:86
  585.3 98.0 %while.20 = (s32[]{:T(128)}, f32[256,2]{0,1:T(2,128)S(1)}, f32[256,2]{0,1:T(2,128)S(1)}, f32[256,128]{0,1:T(8,128)}, s32[64]{0:T(128)S(1)}, /*index=5*/s32[256]{...) while((s32[]{:T(128)}, f32[256,2]{0,1:T(2,128)S(1)}, ...), condition=%wide.region_8.9_spmd.clone, body=%wide.region_4.8_spmd.clone.sunk | while | flops 69780480 | bytes 4175302 | solution.py:100
  607.6 2.2 convolution_add_fusion.2
  632.1 2.2 convolution_add_fusion.2
  656.5 2.2 convolution_add_fusion.2
  681.0 2.2 convolution_add_fusion.2
  (207 shorter events, 104.7 us)
Async XLA Ops:
  6.5 41.0 %copy-start = (bf16[3,720,720]{2,1,0:T(8,128)(2,1)S(1)}, bf16[3,720,720]{2,1,0:T(8,128)(2,1)}, u32[]{:S(2)}) copy-start(bf16[3,720,720]{2,1,0:T(8,128)(2,1)} %param.9) | copy-start | bytes 9331204
  6.5 39.0 %all-gather.12.cloned.1.call-start = ((), (), s32[]{:S(2)}) async-start(), calls=%async_computation | async-start | bytes 1843200 | tf_op jit(solution)/shard_map/all_gather | solution.py:49
  7.3 160.0 %all-gather.18.cloned.1.call-start = ((), (), s32[]{:S(2)}) async-start(), calls=%async_computation.3 | async-start | bytes 3133440 | tf_op jit(solution)/shard_map/all_gather | solution.py:60
  47.4 163.6 %all-gather.20.cloned.1.call-start = ((), (), s32[]{:S(2)}) async-start(), calls=%async_computation.4 | async-start | bytes 1601536 | tf_op jit(solution)/shard_map/all_gather | solution.py:59
  47.5 31.5 %copy-start.6 = (bf16[180,64]{0,1:T(8,128)(2,1)S(1)}, bf16[180,64]{0,1:T(8,128)(2,1)}, u32[]{:S(2)}) copy-start(bf16[180,64]{0,1:T(8,128)(2,1)} %param.12) | copy-start | bytes 69124
  78.3 240.1 %all-gather.22.cloned.1.call-start = ((), (), s32[]{:S(2)}) async-start(), calls=%async_computation.5 | async-start | bytes 1554432 | tf_op jit(solution)/shard_map/all_gather | solution.py:67
  78.9 373.2 %all-gather.16.cloned.1.call-start = ((), (), s32[]{:S(2)}) async-start(), calls=%async_computation.2 | async-start | bytes 1081344 | tf_op jit(solution)/shard_map/all_gather | solution.py:87
  214.5 2.7 copy-start.1
  216.9 1.9 copy-start.2
  218.8 1.1 copy-start.3
  218.8 2.2 copy-start.5
  219.9 1.1 copy-start.4
  221.0 1.3 copy-start.7
  222.3 362.3 %all-gather.14.cloned.1.call-start = ((), (), s32[]{:S(2)}) async-start(), calls=%async_computation.1 | async-start | bytes 1081344 | tf_op jit(solution)/shard_map/all_gather | solution.py:86
  305.2 3.4 copy-start.8
Sparse Core Ops, SparseCore 0:
  9.5 36.0 all-gather.11
  47.6 58.5 all-gather.17
  108.3 56.1 all-gather.19
  167.5 150.8 all-gather.21
  321.1 130.8 all-gather.15
  454.9 129.7 all-gather.13
where the time goes:
time: 694 us; the launch traced here: 692 us
  waiting for transfers between devices  309 us (45%)
  blocking collectives  187 us (27%)
  matrix products  81 us (12%)
  other arithmetic  63.7 us (9%)
  local copies, waits for them, and re-layouts  36.5 us (5%)
  between operations  13.6 us (2%)
    all_gather x1, waiting for transfers between devices, body(): key_piece = lax.all_gather(key_vectors, 'ctx', axis=0, tiled=True)  133 us
    all_gather x1, waiting for transfers between devices, body(): value_piece = lax.all_gather(value_vectors, 'ctx', axis=0, tiled=True)  127 us
    all_gather x1, blocking collectives, body(): value_piece = lax.all_gather(value_weight, 'ctx', axis=0, tiled=True)  83.5 us
    all_gather x1, blocking collectives, body(): key_piece = lax.all_gather(key_weight, 'ctx', axis=0, tiled=True)  78.1 us
    all_gather x1, waiting for transfers between devices, body(): sections = lax.all_gather(hidden, 'segment', axis=0, tiled=True)  38.2 us
    dot_general x16, matrix products, attend_block(): jnp.einsum('tgn,nd->tgd', unscaled.astype(jnp.bfloat16), value_blk, prefe...  35.4 us
    dot_general x16, matrix products, attend_block(): jnp.einsum('tgd,nd->tgn', query_heads, key_blk, preferred_element_type=jn...  34.5 us
    reduce_sum x2, other arithmetic, normalize(): jnp.mean(widened * widened, axis=-1, keepdims=True) + 1e-06  34.3 us
  transfers between devices with their start and end apart: 6, of which 4 were waited for; matrix products, arithmetic and copies ran while one was open for 11% of the time, Pallas kernels for 0%

commit v1 on v0

--- a/solution.py
+++ b/solution.py
@@ -51,7 +51,8 @@
         "ktf,kfc->tc", sections[:3], merge_weight, preferred_element_type=jnp.float32
     )
     col_piece = partial_value.shape[1] // heads_here
-    summed = lax.psum(partial_value, "head")
+    reply = lax.all_gather(partial_value, "head")
+    summed = jnp.sum(reply, axis=0)
     merged_part = lax.dynamic_slice_in_dim(summed, head_id * col_piece, col_piece, 1)
     merged_part = merged_part.astype(jnp.bfloat16)
     embed_part = lax.dynamic_slice_in_dim(sections[3], segment_id * col_piece, col_piece, 1)

time: 694 us -> 741 us (1.068)
  waiting for transfers between devices: 309 us -> 373 us
  blocking collectives: 187 us -> 160 us
    all_gather x0 -> x1, waiting for transfers between devices: none -> 43.7 us  [body(): reply = lax.all_gather(partial_value, 'head')]
    psum x1 -> x0, blocking collectives: 25.7 us -> none  [body(): summed = lax.psum(partial_value, 'head')]
    all_gather x1, waiting for transfers between devices: 9.71 us -> 30.9 us  [body(): query_piece = lax.all_gather(query_weight, 'ctx', axis=0, tiled=True)]
  transfers between devices with their start and end apart: 6 -> 7, of which waited for: 4 -> 5; matrix products, arithmetic and copies ran while one was open for 11% -> 12% of each run, Pallas kernels for 0% -> 0%
where the time goes in v1:
time: 741 us; the launch traced here: 738 us
  waiting for transfers between devices  373 us (50%)
  blocking collectives  160 us (22%)
  matrix products  80.8 us (11%)
  other arithmetic  71 us (10%)
  local copies, waits for them, and re-layouts  39.3 us (5%)
  between operations  13.6 us (2%)
    all_gather x1, waiting for transfers between devices, body(): key_piece = lax.all_gather(key_vectors, 'ctx', axis=0, tiled=True)  133 us
    all_gather x1, waiting for transfers between devices, body(): value_piece = lax.all_gather(value_vectors, 'ctx', axis=0, tiled=True)  126 us
    all_gather x1, blocking collectives, body(): value_piece = lax.all_gather(value_weight, 'ctx', axis=0, tiled=True)  82.7 us
    all_gather x1, blocking collectives, body(): key_piece = lax.all_gather(key_weight, 'ctx', axis=0, tiled=True)  77.4 us
    all_gather x1, waiting for transfers between devices, body(): reply = lax.all_gather(partial_value, 'head')  43.7 us
    all_gather x1, waiting for transfers between devices, body(): sections = lax.all_gather(hidden, 'segment', axis=0, tiled=True)  38.2 us
    dot_general x16, matrix products, attend_block(): jnp.einsum('tgn,nd->tgd', unscaled.astype(jnp.bfloat16), value_blk, prefe...  35.6 us
    reduce_sum x2, other arithmetic, normalize(): jnp.mean(widened * widened, axis=-1, keepdims=True) + 1e-06  34.3 us
  transfers between devices with their start and end apart: 7, of which 5 were waited for; matrix products, arithmetic and copies ran while one was open for 12% of the time, Pallas kernels for 0%

profile of v1, /device:TPU:4, one launch (start us, length us, event | category | flops | bytes accessed | tf_op | source)
XLA Modules:
  0.0 738.5 jit_solution(6835021973550704962)
XLA Ops:
  7.3 38.2 %all-gather.14.cloned.1.call-done = bf16[4,256,720]{1,2,0:T(8,128)(2,1)} async-done(((bf16[1,256,720]{1,2,0:T(8,128)(2,1)}), bf16[4,256,720]{1,2,0:T(8,128)(2,1)}) %all-gather.14.cloned.1.call-update) | async-done | bytes 1474576 | tf_op jit(solution)/shard_map/all_gather | solution.py:49
  45.5 3.5 convolution_bitcast_fusion
  51.1 43.7 %all-gather.22.cloned.1.call-done = f32[1024,720]{0,1:T(8,128)} async-done(((f32[256,720]{0,1:T(8,128)}), f32[1024,720]{0,1:T(8,128)}) %all-gather.22.cloned.1.call-update) | async-done | bytes 2949136 | tf_op jit(solution)/shard_map/all_gather | solution.py:54
  94.8 4.9 reshape.147
  99.7 4.4 reduce_sum.70
  106.3 82.7 %all-gather.5 = bf16[32,180,64]{1,2,0:T(8,128)(2,1)S(1)} all-gather(bf16[1,180,64]{1,2,0:T(8,128)(2,1)S(1)} %bitcast.61), channel_id=1, replica_groups=mesh['segment'=4,'ctx'=32,'head'=4] {'ctx'}, dimensions={0}, use_global_device_ids=true | all-gather | bytes 760320 | tf_op jit(solution)/shard_map/all_gather | solution.py:70
  190.5 3.1 reshape.159
  193.7 31.9 %multiply_reduce_fusion.1 = (f32[256]{0:T(256)S(1)}, f32[256,2880]{0,1:T(8,128)}) fusion(bf16[1,256,2880]{1,0,2:T(2,128)(2,1)} %all-gather.20.cloned.1.call-done), kind=kLoop, calls=%fused_computation.39 | loop fusion | flops 2211584 | bytes 4424704 | tf_op jit(solution)/shard_map/reduce_sum | solution.py:12
  225.6 4.0 reshape.145
  229.6 3.8 copy.26
  233.4 4.1 reshape.144
  237.5 3.2 multiply_convert_fusion.1
  240.7 3.4 reshape.160
  244.1 2.4 multiply_reduce_fusion
  249.6 77.4 %all-gather.3 = bf16[32,180,64]{1,2,0:T(8,128)(2,1)S(1)} all-gather(bf16[1,180,64]{1,2,0:T(8,128)(2,1)S(1)} %bitcast.62), channel_id=1, replica_groups=mesh['segment'=4,'ctx'=32,'head'=4] {'ctx'}, dimensions={0}, use_global_device_ids=true | all-gather | bytes 760320 | tf_op jit(solution)/shard_map/all_gather | solution.py:69
  328.5 3.2 reshape.155
  331.7 3.3 convolution_convert_fusion.2
  335.2 30.9 %all-gather.26.cloned.1.call-done = bf16[32,180,128]{2,1,0:T(8,128)(2,1)} async-done(((bf16[1,180,128]{2,1,0:T(8,128)(2,1)}), bf16[32,180,128]{2,1,0:T(8,128)(2,1)}) %all-gather.26.cloned.1.call-update) | async-done | bytes 1474576 | tf_op jit(solution)/shard_map/all_gather | solution.py:68
  366.1 3.3 reshape.157
  369.4 3.0 convolution_convert_fusion
  372.4 126.4 %all-gather.18.cloned.1.call-done = bf16[8192,64]{0,1:T(8,128)(2,1)} async-done(((bf16[256,64]{0,1:T(8,128)(2,1)}), bf16[8192,64]{0,1:T(8,128)(2,1)}) %all-gather.18.cloned.1.call-update) | async-done | bytes 1048592 | tf_op jit(solution)/shard_map/all_gather | solution.py:88
  498.8 132.7 %all-gather.16.cloned.1.call-done = bf16[8192,64]{0,1:T(8,128)(2,1)} async-done(((bf16[256,64]{0,1:T(8,128)(2,1)}), bf16[8192,64]{0,1:T(8,128)(2,1)}) %all-gather.16.cloned.1.call-update) | async-done | bytes 1048592 | tf_op jit(solution)/shard_map/all_gather | solution.py:87
  632.2 97.8 %while.20 = (s32[]{:T(128)}, f32[256,2]{0,1:T(2,128)S(1)}, f32[256,2]{0,1:T(2,128)S(1)}, f32[256,128]{0,1:T(8,128)}, s32[64]{0:T(128)S(1)}, /*index=5*/s32[256]{...) while((s32[]{:T(128)}, f32[256,2]{0,1:T(2,128)S(1)}, ...), condition=%wide.region_8.9_spmd.clone, body=%wide.region_4.8_spmd.clone.sunk | while | flops 69780480 | bytes 4175302 | solution.py:101
  642.1 2.2 convolution_add_fusion.2
  (209 shorter events, 108.9 us)
Async XLA Ops:
  6.5 39.0 %copy-start = (bf16[3,720,720]{2,1,0:T(8,128)(2,1)S(1)}, bf16[3,720,720]{2,1,0:T(8,128)(2,1)}, u32[]{:S(2)}) copy-start(bf16[3,720,720]{2,1,0:T(8,128)(2,1)} %param.9) | copy-start | bytes 9331204
  6.5 39.0 %all-gather.14.cloned.1.call-start = ((), (), s32[]{:S(2)}) async-start(), calls=%async_computation | async-start | bytes 1843200 | tf_op jit(solution)/shard_map/all_gather | solution.py:49
  7.3 87.5 %all-gather.22.cloned.1.call-start = ((), (), s32[]{:S(2)}) async-start(), calls=%async_computation.4 | async-start | bytes 3686400 | tf_op jit(solution)/shard_map/all_gather | solution.py:54
  49.1 144.6 %all-gather.20.cloned.1.call-start = ((), (), s32[]{:S(2)}) async-start(), calls=%async_computation.3 | async-start | bytes 3133440 | tf_op jit(solution)/shard_map/all_gather | solution.py:61
  51.1 189.6 %all-gather.24.cloned.1.call-start = ((), (), s32[]{:S(2)}) async-start(), calls=%async_computation.5 | async-start | bytes 1601536 | tf_op jit(solution)/shard_map/all_gather | solution.py:60
  99.7 6.6 copy-start.5
  105.6 260.5 %all-gather.26.cloned.1.call-start = ((), (), s32[]{:S(2)}) async-start(), calls=%async_computation.6 | async-start | bytes 1554432 | tf_op jit(solution)/shard_map/all_gather | solution.py:68
  106.2 392.6 %all-gather.18.cloned.1.call-start = ((), (), s32[]{:S(2)}) async-start(), calls=%async_computation.2 | async-start | bytes 1081344 | tf_op jit(solution)/shard_map/all_gather | solution.py:88
  244.1 2.7 copy-start.1
  246.5 1.7 copy-start.2
  246.5 1.8 copy-start.4
  247.0 1.2 copy-start.3
  248.3 1.3 copy-start.6
  249.5 382.0 %all-gather.16.cloned.1.call-start = ((), (), s32[]{:S(2)}) async-start(), calls=%async_computation.1 | async-start | bytes 1081344 | tf_op jit(solution)/shard_map/all_gather | solution.py:87
  331.7 3.4 copy-start.7
Sparse Core Ops, SparseCore 0:
  9.5 36.0 all-gather.13
  49.2 45.5 all-gather.21
  96.9 58.1 all-gather.19
  157.1 57.1 all-gather.23
  217.3 148.7 all-gather.25
  368.8 129.9 all-gather.17
  501.7 129.7 all-gather.15
